TPU v7x, 256 devices: a whole 4x4x8 slice. The times are simulated.
256 devices in a mesh: ax: 4 (over z_lo), rad: 8 (over y, core), az: 8 (over x, z_hi).
Axes of the slice: x: 4, y: 4, z: 8 (z_hi: 2, z_lo: 4; z = z_hi * 4 + z_lo), core: 2. Of those that a mesh axis runs over, the one named last changes fastest.
Arguments:
- positions: float32 [3, 4, 8, 131072], P(None, 'ax', 'rad', 'az'), may hold values from 0 to 0.1
- velocity: float32 [3, 4, 8, 131072], P(None, 'ax', 'rad', 'az'), may hold values from -6 to 6
- diameter: float32 [4, 8, 131072], P('ax', 'rad', 'az'), may hold values from 0.02 to 0.1
- cell_index: int32 [4, 8, 131072], P('ax', 'rad', 'az'), may hold values from 0 to 32767
- pair_list: int32 [2, 4, 8, 262144], P(None, 'ax', 'rad', 'az'), may hold values from 0 to 34815, as said below
- live_pairs: int32 [4, 8, 8], P('ax', 'rad', 'az'), may hold values from 8192 to 32768, as said below
- gas_velocity: float32 [3, 32, 128, 2048], P(None, 'ax', 'rad', 'az'), may hold values from -6 to 6
Outputs:
- disturbance: float32 [3, 4, 8, 131072], P(None, 'ax', 'rad', 'az')
- drag_source: float32 [3, 32, 128, 2048], P(None, 'ax', 'rad', 'az')
Inputs may be any that keep to these rules, and one draw needn't show every extreme that they name: pair_list[0] is an own droplet, under 16384; a partner on a neighbouring device lies among that device's last 2048 droplets (q from 14336) or first 2048 droplets (q under 2 * 16384 + 2048); an own partner differs from the first droplet. `live_pairs`: slots at and beyond the count are padding and are ignored.
All inputs are finite; a program needn't handle non-finite values.
Results may differ from a plain program's by a relative error of at most 0.0003.
Values sent between devices are 32-bit elements; how exact they have to be, the bound alone decides.
No kernel may reach another device: no remote copies, remote signals or barrier semaphores. Data moves between devices by JAX's collectives and lax.ppermute only.
A program may use at most 128 MiB of HBM per device.

v0:
```python
import jax
import jax.numpy as jnp
from jax import lax
from jax.sharding import PartitionSpec as P

piep_coef = 1.0
drag_coef = 20.0


def with_halo(x, sides, width, wrap):
    for axis, dim in sides:
        count, length = (lax.axis_size(axis), x.shape[dim])
        up = [(i, (i + 1) % count) for i in range(count if wrap else count - 1)]
        down = [(j, i) for i, j in up]
        last = lax.slice_in_dim(x, length - width, length, axis=dim)
        leading = lax.slice_in_dim(x, 0, width, axis=dim)
        before = lax.ppermute(last, axis, up)
        after = lax.ppermute(leading, axis, down)
        x = jnp.concatenate([before, x, after], axis=dim)
    return x


def from_behind(x, axis, by):
    count = lax.axis_size(axis)
    return lax.ppermute(x, axis, [(i, (i + by) % count) for i in range(count)])


def gauss_taps():
    offsets = jnp.arange(-2, 3).astype(jnp.float32)
    raw_taps = jnp.exp(-0.5 * offsets * offsets)
    return raw_taps / jnp.sum(raw_taps)


def reach_weight(radius, squared_gap):
    spread = squared_gap + radius * radius
    return radius * radius * radius / (spread * jnp.sqrt(spread))


def taps_valid(padded, axis_number, kernel_taps):
    out_length = padded.shape[axis_number] - 4
    total = jnp.zeros(
        padded.shape[:axis_number] + (out_length,) + padded.shape[axis_number + 1 :], jnp.float32
    )
    for tap_number in range(5):
        total = total + kernel_taps[tap_number] * lax.slice_in_dim(
            padded, tap_number, tap_number + out_length, axis=axis_number
        )
    return total


def pair_sweep(own_state, shell_state, pair_list, live_pairs, offset, margin):
    pair_total = pair_list.shape[3]
    block_size = min(4096, pair_total)
    pair_rows = pair_list.reshape(2, pair_total)
    live_total = live_pairs.reshape(())
    block_count = (live_total + block_size - 1) // block_size
    empty_sums = jnp.zeros((3, shell_state.shape[1]), jnp.float32)

    def one_block(block_number, accumulated):
        block_start = block_number * block_size
        block_rows = lax.dynamic_slice_in_dim(pair_rows, block_start, block_size, 1)
        head_index = block_rows[0]
        tail_index = block_rows[1] - offset
        live_mask = (block_start + jnp.arange(block_size) < live_total).astype(jnp.float32)
        near_state = jnp.take(own_state, head_index, axis=1)
        far_state = jnp.take(shell_state, tail_index, axis=1)
        separation = far_state[0:3] - near_state[0:3]
        squared_gap = jnp.sum(separation * separation, axis=0)
        weight_far = reach_weight(far_state[6], squared_gap)
        weight_near = reach_weight(near_state[6], squared_gap)
        to_head = piep_coef * (weight_far * live_mask)[None] * far_state[3:6]
        to_tail = piep_coef * (weight_near * live_mask)[None] * near_state[3:6]
        accumulated = accumulated.at[:, head_index + margin].add(to_head)
        return accumulated.at[:, tail_index].add(to_tail)

    return lax.fori_loop(0, block_count, one_block, empty_sums)


def per_device(positions, velocity, diameter, cell_index, pair_list, live_pairs, gas_velocity):
    droplet_count = positions.shape[3]
    cells_ax, cells_rad, cells_az = (
        gas_velocity.shape[1],
        gas_velocity.shape[2],
        gas_velocity.shape[3],
    )
    cell_total = cells_ax * cells_rad * cells_az
    gas_flat = gas_velocity.reshape(3, cell_total)
    cell_ids = cell_index.reshape(droplet_count)
    seen_gas = jnp.take(gas_flat, cell_ids, axis=1)
    slip_velocity = seen_gas - velocity.reshape(3, droplet_count)
    diam_row = diameter.reshape(1, droplet_count)
    radius = 0.5 * diam_row
    own_state = jnp.concatenate(
        [positions.reshape(3, droplet_count), slip_velocity, radius], axis=0
    )
    shell_state = with_halo(own_state, (("az", 1),), droplet_count, True)
    accumulated = pair_sweep(own_state, shell_state, pair_list, live_pairs, 0, droplet_count)
    from_lower = from_behind(accumulated[:, droplet_count + droplet_count :], "az", 1)
    from_upper = from_behind(accumulated[:, :droplet_count], "az", -1)
    correction = accumulated[:, droplet_count : droplet_count + droplet_count]
    correction = correction.at[:, :droplet_count].add(from_lower)
    correction = correction.at[:, droplet_count - droplet_count :].add(from_upper)
    force = drag_coef * diam_row * (slip_velocity + correction)
    deposit = jnp.zeros((3, cell_total), jnp.float32).at[:, cell_ids].add(-force)
    deposit = deposit.reshape(3, cells_ax, cells_rad, cells_az)
    kernel_taps = gauss_taps()
    padded = with_halo(deposit, (("ax", 1), ("rad", 2)), 2, False)
    padded = with_halo(padded, (("az", 3),), 2, True)
    smoothed = taps_valid(padded, 1, kernel_taps)
    smoothed = taps_valid(smoothed, 2, kernel_taps)
    smoothed = taps_valid(smoothed, 3, kernel_taps)
    return (correction.reshape(3, 1, 1, droplet_count), smoothed)


def solution(mesh):
    return jax.shard_map(
        per_device,
        mesh=mesh,
        in_specs=(
            P(None, "ax", "rad", "az"),
            P(None, "ax", "rad", "az"),
            P("ax", "rad", "az"),
            P("ax", "rad", "az"),
            P(None, "ax", "rad", "az"),
            P("ax", "rad", "az"),
            P(None, "ax", "rad", "az"),
        ),
        out_specs=(P(None, "ax", "rad", "az"), P(None, "ax", "rad", "az")),
        check_vma=False,
    )
```

profile of v0, /device:TPU:40, one launch (start us, length us, event | category | flops | bytes accessed | tf_op | source)
XLA Modules:
  0.0 1243.1 jit_solution(3880548067701903286)
XLA Ops:
  0.6 9.5 copy.46
  10.3 60.6 %gather_fusion.2 = f32[16384,3]{1,0:T(8,128)} fusion(f32[3,32768]{0,1:T(8,128)} %bitcast.81, s32[16384]{0:T(1024)S(1)} %broadcast_clamp_fusion.2), kind=kCustom, calls=%fused_computation.2 | custom fusion | bytes 458752 | tf_op jit(solution)/shard_map/jit(_take)/gather | solution.py:89
  77.1 8.6 collective-permute-start.1
  91.8 27.2 %collective-permute-done.1 = f32[7,16384]{1,0:T(8,128)S(1)} collective-permute-done((f32[7,16384]{1,0:T(8,128)S(1)}, f32[7,16384]{1,0:T(8,128)S(1)}, u32[]{:S(2)}, u32[]{:S(2)}) %collective-permute-start.1) | collective-permute-done | bytes 458784 | tf_op jit(solution)/shard_map/ppermute | solution.py:18
  119.8 11.7 collective-permute-done
  133.0 13.1 %copy.48 = f32[7,49152]{0,1:T(8,128)} copy(f32[7,49152]{1,0:T(8,128)S(1)} %pad_maximum_fusion) | data formatting | bytes 2752512 | tf_op jit(solution)/shard_map/while | solution.py:76
  146.1 8.5 broadcast_in_dim.48
  154.6 439.8 %while.16 = (s32[]{:T(128)}, f32[3,49152]{0,1:T(8,128)}, s32[]{:T(128)}, s32[2,32768]{1,0:T(2,128)S(1)}, s32[]{:T(128)}, /*index=5*/f32[7,49152]{0,1:T(8,128)}, ...) while((s32[]{:T(128)}, f32[3,49152]{0,1:T(8,128)}, s32[]{:T(128)}, ...), condition=%wide.region_4.5_spmd, body=%wide.region_0.4_spmd.sunk | while | flops 294919 | bytes 2605255 | solution.py:76
  154.8 14.1 %gather_fusion = f32[4096,7]{1,0:T(8,128)S(1)} fusion(f32[7,16384]{0,1:T(8,128)} %get-tuple-element.288, s32[4096]{0:T(1024)S(1)} %broadcast_clamp_fusion.5), kind=kCustom, calls=%fused_computation.1.clone.1 | custom fusion | bytes 245760 | tf_op jit(solution)/shard_map/while/body/jit(_take)/gather | solution.py:65
  169.6 18.9 %gather_fusion.1 = f32[4096,7]{1,0:T(8,128)S(1)} fusion(f32[7,49152]{0,1:T(8,128)} %get-tuple-element.287, s32[4096]{0:T(1024)S(1)} %broadcast_clamp_fusion.6), kind=kCustom, calls=%fused_computation.clone.1 | custom fusion | bytes 245760 | tf_op jit(solution)/shard_map/while/body/jit(_take)/gather | solution.py:66
  190.8 36.6 %scatter_fusion = f32[3,49152]{0,1:T(8,128)} fusion(f32[3,49152]{0,1:T(8,128)} %get-tuple-element.271, s32[4096]{0:T(1024)S(1)} %bitcast.87, f32[4096,3]{1,0:T(8,128)S(1)} %copy.72), kind=kCustom, calls=%fused_computation.3.clone.1 | custom fusion | flops 12288 | bytes 163840 | tf_op jit(solution)/shard_map/while/body/scatter-add | solution.py:73
  228.0 36.6 %scatter_fusion.1 = f32[3,49152]{0,1:T(8,128)} fusion(f32[3,49152]{0,1:T(8,128)} %scatter_fusion, s32[4096]{0:T(1024)S(1)} %bitcast.83, f32[4096,3]{1,0:T(8,128)S(1)} %copy.73), kind=kCustom, calls=%fused_computation.4.clone.1 | custom fusion | flops 12288 | bytes 163840 | tf_op jit(solution)/shard_map/while/body/scatter-add | solution.py:74
  264.7 14.1 %gather_fusion = f32[4096,7]{1,0:T(8,128)S(1)} fusion(f32[7,16384]{0,1:T(8,128)} %get-tuple-element.288, s32[4096]{0:T(1024)S(1)} %broadcast_clamp_fusion.5), kind=kCustom, calls=%fused_computation.1.clone.1 | custom fusion | bytes 245760 | tf_op jit(solution)/shard_map/while/body/jit(_take)/gather | solution.py:65
  279.5 18.9 %gather_fusion.1 = f32[4096,7]{1,0:T(8,128)S(1)} fusion(f32[7,49152]{0,1:T(8,128)} %get-tuple-element.287, s32[4096]{0:T(1024)S(1)} %broadcast_clamp_fusion.6), kind=kCustom, calls=%fused_computation.clone.1 | custom fusion | bytes 245760 | tf_op jit(solution)/shard_map/while/body/jit(_take)/gather | solution.py:66
  300.7 36.6 %scatter_fusion = f32[3,49152]{0,1:T(8,128)} fusion(f32[3,49152]{0,1:T(8,128)} %get-tuple-element.271, s32[4096]{0:T(1024)S(1)} %bitcast.87, f32[4096,3]{1,0:T(8,128)S(1)} %copy.72), kind=kCustom, calls=%fused_computation.3.clone.1 | custom fusion | flops 12288 | bytes 163840 | tf_op jit(solution)/shard_map/while/body/scatter-add | solution.py:73
  338.0 36.6 %scatter_fusion.1 = f32[3,49152]{0,1:T(8,128)} fusion(f32[3,49152]{0,1:T(8,128)} %scatter_fusion, s32[4096]{0:T(1024)S(1)} %bitcast.83, f32[4096,3]{1,0:T(8,128)S(1)} %copy.73), kind=kCustom, calls=%fused_computation.4.clone.1 | custom fusion | flops 12288 | bytes 163840 | tf_op jit(solution)/shard_map/while/body/scatter-add | solution.py:74
  374.7 14.2 %gather_fusion = f32[4096,7]{1,0:T(8,128)S(1)} fusion(f32[7,16384]{0,1:T(8,128)} %get-tuple-element.288, s32[4096]{0:T(1024)S(1)} %broadcast_clamp_fusion.5), kind=kCustom, calls=%fused_computation.1.clone.1 | custom fusion | bytes 245760 | tf_op jit(solution)/shard_map/while/body/jit(_take)/gather | solution.py:65
  389.5 18.9 %gather_fusion.1 = f32[4096,7]{1,0:T(8,128)S(1)} fusion(f32[7,49152]{0,1:T(8,128)} %get-tuple-element.287, s32[4096]{0:T(1024)S(1)} %broadcast_clamp_fusion.6), kind=kCustom, calls=%fused_computation.clone.1 | custom fusion | bytes 245760 | tf_op jit(solution)/shard_map/while/body/jit(_take)/gather | solution.py:66
  410.7 36.6 %scatter_fusion = f32[3,49152]{0,1:T(8,128)} fusion(f32[3,49152]{0,1:T(8,128)} %get-tuple-element.271, s32[4096]{0:T(1024)S(1)} %bitcast.87, f32[4096,3]{1,0:T(8,128)S(1)} %copy.72), kind=kCustom, calls=%fused_computation.3.clone.1 | custom fusion | flops 12288 | bytes 163840 | tf_op jit(solution)/shard_map/while/body/scatter-add | solution.py:73
  447.9 36.6 %scatter_fusion.1 = f32[3,49152]{0,1:T(8,128)} fusion(f32[3,49152]{0,1:T(8,128)} %scatter_fusion, s32[4096]{0:T(1024)S(1)} %bitcast.83, f32[4096,3]{1,0:T(8,128)S(1)} %copy.73), kind=kCustom, calls=%fused_computation.4.clone.1 | custom fusion | flops 12288 | bytes 163840 | tf_op jit(solution)/shard_map/while/body/scatter-add | solution.py:74
  484.6 14.1 %gather_fusion = f32[4096,7]{1,0:T(8,128)S(1)} fusion(f32[7,16384]{0,1:T(8,128)} %get-tuple-element.288, s32[4096]{0:T(1024)S(1)} %broadcast_clamp_fusion.5), kind=kCustom, calls=%fused_computation.1.clone.1 | custom fusion | bytes 245760 | tf_op jit(solution)/shard_map/while/body/jit(_take)/gather | solution.py:65
  499.4 18.9 %gather_fusion.1 = f32[4096,7]{1,0:T(8,128)S(1)} fusion(f32[7,49152]{0,1:T(8,128)} %get-tuple-element.287, s32[4096]{0:T(1024)S(1)} %broadcast_clamp_fusion.6), kind=kCustom, calls=%fused_computation.clone.1 | custom fusion | bytes 245760 | tf_op jit(solution)/shard_map/while/body/jit(_take)/gather | solution.py:66
  520.6 36.6 %scatter_fusion = f32[3,49152]{0,1:T(8,128)} fusion(f32[3,49152]{0,1:T(8,128)} %get-tuple-element.271, s32[4096]{0:T(1024)S(1)} %bitcast.87, f32[4096,3]{1,0:T(8,128)S(1)} %copy.72), kind=kCustom, calls=%fused_computation.3.clone.1 | custom fusion | flops 12288 | bytes 163840 | tf_op jit(solution)/shard_map/while/body/scatter-add | solution.py:73
  557.8 36.6 %scatter_fusion.1 = f32[3,49152]{0,1:T(8,128)} fusion(f32[3,49152]{0,1:T(8,128)} %scatter_fusion, s32[4096]{0:T(1024)S(1)} %bitcast.83, f32[4096,3]{1,0:T(8,128)S(1)} %copy.73), kind=kCustom, calls=%fused_computation.4.clone.1 | custom fusion | flops 12288 | bytes 163840 | tf_op jit(solution)/shard_map/while/body/scatter-add | solution.py:74
  594.4 13.8 %copy.50 = f32[3,49152]{1,0:T(4,128)S(1)} copy(f32[3,49152]{0,1:T(8,128)} %get-tuple-element.134) | data formatting | bytes 1179648 | tf_op jit(solution)/shard_map/while | solution.py:76
  608.4 5.9 collective-permute-start.2
  618.7 335.8 %collective-permute-done.2 = f32[3,16384]{1,0:T(4,128)S(1)} collective-permute-done((f32[3,16384]{1,0:T(4,128)S(1)}, f32[3,16384]{1,0:T(4,128)S(1)}, u32[]{:S(2)}, u32[]{:S(2)}) %collective-permute-start.2) | collective-permute-done | bytes 196640 | tf_op jit(solution)/shard_map/ppermute | solution.py:25
  959.7 94.4 %scatter_custom_fusion.2 = f32[3,32768]{0,1:T(8,128)} fusion(s32[16384]{0:T(1024)S(1)} %bitcast.97, f32[16384,3]{1,0:T(8,128)} %copy.53, f32[]{:T(128)} %constant.188.clone.1), kind=kCustom, calls=%fused_computation.37 | custom fusion | flops 49152 | bytes 393728 | tf_op jit(solution)/shard_map/scatter-add | solution.py:104
  1054.1 10.0 copy.54
  1064.1 119.9 %collective-permute-start.5 = (f32[3,2,16,256]{3,2,1,0:T(8,128)S(1)}, f32[3,2,16,256]{3,2,1,0:T(8,128)S(1)}, u32[]{:S(2)}, u32[]{:S(2)}) collective-permute-start(f32[3,2,16,256]{3,2,1,0:T(8,128)S(1)} %get-tuple-element.190), channel_id=1, source_target_pairs={{64,0},{128,64},{192,128},{65,1},{129,65},{193,129},{66,2},{130,66... | collective-permute-start | bytes 294920 | tf_op jit(solution)/shard_map/ppermute | solution.py:18
  1198.6 5.9 collective-permute-start.8
  1206.0 19.8 %collective-permute-done.9 = f32[3,12,20,2]{3,2,1,0:T(8,128)S(1)} collective-permute-done((f32[3,12,20,2]{3,2,1,0:T(8,128)S(1)}, f32[3,12,20,2]{3,2,1,0:T(8,128)S(1)}, u32[]{:S(2)}, u32[]{:S(2)}) %collective-permute-start.9) | collective-permute-done | bytes 5792 | tf_op jit(solution)/shard_map/ppermute | solution.py:18
  (110 shorter events, 71.8 us)
Async XLA Ops:
  0.6 9.6 copy-start.1
  70.8 5.5 copy-start.5
  70.8 5.7 copy-start.3
  70.8 5.8 copy-start.4
  77.1 42.0 %collective-permute-start.1 = (f32[7,16384]{1,0:T(8,128)S(1)}, f32[7,16384]{1,0:T(8,128)S(1)}, u32[]{:S(2)}, u32[]{:S(2)}) collective-permute-start(f32[7,16384]{1,0:T(8,128)S(1)} %pad_maximum_fusion.3), channel_id=1, source_target_pairs={{1,0},{2,1},{3,2},{4,3},{5,4},{6,5},{7,6},{0,7},{9,8},{10,9},{11,1... | collective-permute-start | bytes 1376264 | tf_op jit(solution)/shard_map/ppermute | solution.py:18
  85.6 45.9 %collective-permute-start = (f32[7,16384]{1,0:T(8,128)S(1)}, f32[7,16384]{1,0:T(8,128)}, u32[]{:S(2)}, u32[]{:S(2)}) collective-permute-start(f32[7,16384]{1,0:T(8,128)S(1)} %pad_maximum_fusion.3), channel_id=1, source_target_pairs={{0,1},{1,2},{2,3},{3,4},{4,5},{5,6},{6,7},{7,0},{8,9},{9,10},{10,1... | collective-permute-start | bytes 1376264 | tf_op jit(solution)/shard_map/ppermute | solution.py:17
  86.3 5.3 copy-start.2
  119.0 0.8 copy-start
  608.3 10.4 collective-permute-start.3
  608.4 346.0 %collective-permute-start.2 = (f32[3,16384]{1,0:T(4,128)S(1)}, f32[3,16384]{1,0:T(4,128)S(1)}, u32[]{:S(2)}, u32[]{:S(2)}) collective-permute-start(f32[3,16384]{1,0:T(4,128)S(1)} %get-tuple-element.185), channel_id=1, source_target_pairs={{0,1},{1,2},{2,3},{3,4},{4,5},{5,6},{6,7},{7,0},{8,9},{9,10},{10,1... | collective-permute-start | bytes 589832 | tf_op jit(solution)/shard_map/ppermute | solution.py:25
  1064.1 124.1 %collective-permute-start.5 = (f32[3,2,16,256]{3,2,1,0:T(8,128)S(1)}, f32[3,2,16,256]{3,2,1,0:T(8,128)S(1)}, u32[]{:S(2)}, u32[]{:S(2)}) collective-permute-start(f32[3,2,16,256]{3,2,1,0:T(8,128)S(1)} %get-tuple-element.190), channel_id=1, source_target_pairs={{64,0},{128,64},{192,128},{65,1},{129,65},{193,129},{66,2},{130,66... | collective-permute-start | bytes 294920 | tf_op jit(solution)/shard_map/ppermute | solution.py:18
  1184.0 6.5 collective-permute-start.4
  1190.5 5.0 collective-permute-start.7
  1192.5 5.7 collective-permute-start.6
  1198.4 27.3 %collective-permute-start.9 = (f32[3,12,20,2]{3,2,1,0:T(8,128)S(1)}, f32[3,12,20,2]{3,2,1,0:T(8,128)S(1)}, u32[]{:S(2)}, u32[]{:S(2)}) collective-permute-start(f32[3,12,20,2]{3,2,1,0:T(8,128)S(1)} %get-tuple-element.184), channel_id=1, source_target_pairs={{1,0},{2,1},{3,2},{4,3},{5,4},{6,5},{7,6},{0,7},{9,8},{10,9},{11,1... | collective-permute-start | bytes 17288 | tf_op jit(solution)/shard_map/ppermute | solution.py:18
  1198.6 32.7 %collective-permute-start.8 = (f32[3,12,20,2]{3,2,1,0:T(8,128)S(1)}, f32[3,12,20,2]{3,2,1,0:T(8,128)S(1)}, u32[]{:S(2)}, u32[]{:S(2)}) collective-permute-start(f32[3,12,20,2]{3,2,1,0:T(8,128)S(1)} %get-tuple-element.183), channel_id=1, source_target_pairs={{0,1},{1,2},{2,3},{3,4},{4,5},{5,6},{6,7},{7,0},{8,9},{9,10},{10,1... | collective-permute-start | bytes 17288 | tf_op jit(solution)/shard_map/ppermute | solution.py:17
where the time goes:
time: 1250 us; the launch traced here: 1240 us
  waiting for transfers between devices  409 us (33%)
  other arithmetic  407 us (33%)
  local copies, waits for them, and re-layouts  277 us (22%)
  starting transfers between devices  148 us (12%)
    ppermute x2, waiting for transfers between devices, from_behind(): return lax.ppermute(x, axis, [(i, (i + by) % count) for i in range(count)])  340 us
    scatter-add x4, other arithmetic, one_block(): return accumulated.at[:, tail_index].add(to_tail)  146 us
    scatter-add x4, other arithmetic, one_block(): accumulated = accumulated.at[:, head_index + margin].add(to_head)  146 us
    ppermute x4, starting transfers between devices, with_halo(): after = lax.ppermute(leading, axis, down)  130 us
    scatter-add x1, other arithmetic, per_device(): jnp.zeros((3, cell_total), jnp.float32).at[:, cell_ids].add(-force)  94.4 us
    gather x8, local copies, waits for them, and re-layouts, one_block(): far_state = jnp.take(shell_state, tail_index, axis=1)  78.2 us
    gather x2, local copies, waits for them, and re-layouts, per_device(): seen_gas = jnp.take(gas_flat, cell_ids, axis=1)  66.1 us
    gather x8, local copies, waits for them, and re-layouts, one_block(): near_state = jnp.take(own_state, head_index, axis=1)  59.1 us
  transfers between devices with their start and end apart: 10, of which 8 were waited for; matrix products, arithmetic and copies ran while one was open for 1% of the time, Pallas kernels for 0%

commit v1 on v0

v1 whole, which is shorter than its diff:
```python
import jax
import jax.numpy as jnp
from jax import lax
from jax.experimental import pallas as pl
from jax.experimental.pallas import tpu as pltpu
from jax.sharding import PartitionSpec as P

piep_coef = 1.0
drag_coef = 20.0

LANES = 128
ROWS = 8
BLOCK = 2048
BAND_BLOCKS = 16
GAS_STEP = 5
HEAD_STEP = 6
DEAD = 1 << 29

NT = (((1,), (1,)), ((), ()))
ANY = pl.ANY
VMEM = pltpu.VMEM
SMEM = pltpu.SMEM


def params(megabytes=40):
    return pltpu.CompilerParams(vmem_limit_bytes=megabytes << 20)


def lane_gather(table, index):
    numbers = lax.GatherDimensionNumbers(
        offset_dims=(),
        collapsed_slice_dims=(1,),
        start_index_map=(1,),
        operand_batching_dims=(0,),
        start_indices_batching_dims=(0,),
    )
    return lax.gather(
        table,
        index[..., None],
        numbers,
        slice_sizes=(1, 1),
        mode=lax.GatherScatterMode.PROMISE_IN_BOUNDS,
    )


def sort_network(regs, place, levels):
    sub = lax.broadcasted_iota(jnp.int32, (ROWS, LANES), 0)
    lane = lax.broadcasted_iota(jnp.int32, (ROWS, LANES), 1)
    count = len(regs)

    def bit_fill(bit, v):
        if bit >= levels:
            return 0
        kind, k = place[bit]
        if kind == "v":
            return -((v >> k) & 1)
        return -(((sub if kind == "s" else lane) >> k) & 1)

    flip = [0] * count
    for level in range(1, levels + 1):
        fills = {}
        for v in range(count):
            kind, k = place[level] if level < levels else ("v", 99)
            key = (v >> k) & 1 if kind == "v" else 0
            if key not in fills:
                fills[key] = bit_fill(level, v)
            new = fills[key]
            if isinstance(new, int) and isinstance(flip[v], int):
                if new != flip[v]:
                    regs[v] = ~regs[v]
            else:
                regs[v] = regs[v] ^ (new ^ flip[v])
            flip[v] = new
        for bit in reversed(range(level)):
            kind, k = place[bit]
            step = 1 << k
            if kind == "v":
                for v in range(count):
                    if not v & step:
                        a, b = regs[v], regs[v | step]
                        regs[v], regs[v | step] = jnp.minimum(a, b), jnp.maximum(a, b)
            else:
                axis, size, where = (0, ROWS, sub) if kind == "s" else (1, LANES, lane)
                lower = (where & step) == 0
                for v in range(count):
                    x = regs[v]
                    ahead = pltpu.roll(x, size - step, axis)
                    behind = ahead if 2 * step == size else pltpu.roll(x, step, axis)
                    regs[v] = jnp.where(lower, jnp.minimum(x, ahead), jnp.maximum(x, behind))
    return regs


def split_two(x):
    high = x.astype(jnp.bfloat16).astype(jnp.float32)
    return high, x - high


def split_three(x):
    high, rest = split_two(x)
    mid, low = split_two(rest)
    return high, mid, low


def packed_row(ref, row):
    return jnp.broadcast_to(ref[row : row + 1, :], (16, LANES)).astype(jnp.bfloat16)


def one_hot_rows(low, count, iota16):
    one = jnp.ones((16, LANES), jnp.bfloat16)
    zero = jnp.zeros((16, LANES), jnp.bfloat16)
    return jnp.concatenate(
        [jnp.where(low - float(16 * k) == iota16, one, zero) for k in range(count // 16)], axis=0
    )


def spread_rows(rel, parts, iota16):
    hit = rel == iota16
    zero = jnp.zeros((16, LANES), jnp.bfloat16)
    return jnp.concatenate(
        [jnp.concatenate([jnp.where(hit, p, zero) for p in part], axis=1) for part in parts], axis=0
    )


def row_iota():
    return lax.broadcasted_iota(jnp.int32, (16, LANES), 0).astype(jnp.float32).astype(jnp.bfloat16)


def droplet_kernel(
    cell_ref, gas_ref, pos_ref, vel_ref, diam_ref,
    table_ref, keys_ref, ends_ref,
    gas_rows, flipped, ends_smem, seen, idx, val, sem,
):
    regs = []
    sub = lax.broadcasted_iota(jnp.int32, (ROWS, LANES), 0)
    lane = lax.broadcasted_iota(jnp.int32, (ROWS, LANES), 1)
    for v in range(16):
        own = (v % 2) * 1024 + sub * LANES + lane
        regs.append(cell_ref[v * ROWS : (v + 1) * ROWS, :] * BLOCK + own)
    place = [("l", k) for k in range(7)] + [("s", k) for k in range(3)] + [("v", 0)]
    regs = sort_network(regs, place, 11)
    keys = jnp.concatenate(regs, axis=0)
    keys_ref[...] = keys
    turned = lax.shift_right_logical(keys, 19).T
    flipped[0:8, :] = turned[0:8, :]
    flipped[8:16, :] = turned[120:128, :]
    ends_ref[...] = flipped[...]
    copy = pltpu.make_async_copy(flipped, ends_smem, sem)
    copy.start()
    for r in range(16):
        rows = slice(r * ROWS, (r + 1) * ROWS)
        for c in range(3):
            for half in range(2):
                gas_rows[rows, half * 4 + c, :] = gas_ref[c, rows, half * LANES : (half + 1) * LANES]
    copy.wait()
    iota16 = row_iota()

    def one_block(db, carry):
        group_rows = pl.ds(pl.multiple_of(db * 16, 16), 16)
        group_keys = keys_ref[group_rows, :]
        idx[0] = lax.shift_right_logical(group_keys, 19)
        idx[1] = lax.shift_right_logical(group_keys, 11) & (LANES - 1)
        idx[2] = lax.shift_right_logical(group_keys, 18) & 1
        firsts = [ends_smem[0, db * 16 + g] for g in range(16)]
        trips = jnp.int32(0)
        for g in range(16):
            trips = jnp.maximum(trips, ends_smem[15, db * 16 + g] - firsts[g])
        trips = trips // GAS_STEP + 1

        def one_trip(t, found):
            out = []
            for g in range(16):
                row = jnp.broadcast_to(idx[0, g : g + 1, :], (ROWS, LANES))
                low = jnp.broadcast_to(idx[1, g : g + 1, :], (ROWS, LANES))
                base = jnp.minimum(firsts[g] + t * GAS_STEP, LANES)
                total = found[g]
                for u in range(GAS_STEP):
                    got = lane_gather(gas_rows[base + u], low)
                    total = jnp.where(row == base + u, got, total)
                out.append(total)
            return tuple(out)

        found = lax.fori_loop(
            0, trips, one_trip, tuple(jnp.zeros((ROWS, LANES), jnp.float32) for _ in range(16))
        )
        for g in range(16):
            upper = jnp.broadcast_to(idx[2, g : g + 1, :], (ROWS, LANES)) == 1
            seen[g] = jnp.where(upper, pltpu.roll(found[g], 4, 0), found[g])
        place_in = group_keys & (BLOCK - 1)
        val[0] = lax.shift_right_logical(place_in, 7).astype(jnp.float32)
        val[1] = (place_in & (LANES - 1)).astype(jnp.float32)
        for c in range(3):
            for n, part in enumerate(split_three(seen[:, c, :])):
                val[2 + 3 * c + n] = part
        total = jnp.zeros((48, LANES), jnp.float32)
        for g in range(16):
            rel = packed_row(val.at[0], g)
            hot = one_hot_rows(packed_row(val.at[1], g), LANES, iota16)
            parts = [[packed_row(val.at[2 + 3 * c + n], g) for n in range(3)] for c in range(3)]
            total = total + lax.dot_general(
                spread_rows(rel, parts, iota16),
                jnp.concatenate([hot, hot, hot], axis=1),
                NT,
                preferred_element_type=jnp.float32,
            )
        for c in range(3):
            table_ref[group_rows, c, :] = pos_ref[c, group_rows, :]
            table_ref[group_rows, 3 + c, :] = total[16 * c : 16 * c + 16] - vel_ref[c, group_rows, :]
        table_ref[group_rows, 6, :] = 0.5 * diam_ref[group_rows, :]
        table_ref[group_rows, 7, :] = jnp.zeros((16, LANES), jnp.float32)
        return carry

    lax.fori_loop(0, 8, one_block, 0)


def droplet_states(cells, gas, pos, vel, diam):
    f32, i32 = jnp.float32, jnp.int32
    return pl.pallas_call(
        droplet_kernel,
        name="droplet_states",
        out_shape=(
            jax.ShapeDtypeStruct((128, ROWS, LANES), f32),
            jax.ShapeDtypeStruct((128, LANES), i32),
            jax.ShapeDtypeStruct((16, LANES), i32),
        ),
        scratch_shapes=[
            VMEM((144, ROWS, LANES), f32),
            VMEM((16, LANES), i32),
            SMEM((16, LANES), i32),
            VMEM((16, ROWS, LANES), f32),
            VMEM((3, 16, LANES), i32),
            VMEM((11, 16, LANES), f32),
            pltpu.SemaphoreType.DMA,
        ],
        compiler_params=params(),
    )(cells, gas, pos, vel, diam)


def pair_sort_kernel(live_ref, pairs_ref, keys_ref, ends_ref):
    live = live_ref[0, 0]
    sub = lax.broadcasted_iota(jnp.int32, (ROWS, LANES), 0)
    lane = lax.broadcasted_iota(jnp.int32, (ROWS, LANES), 1)
    regs = []
    for v in range(32):
        rows = slice(v * ROWS, (v + 1) * ROWS)
        slot = v * 1024 + sub * LANES + lane
        head = pairs_ref[0, rows, :]
        tail = pairs_ref[1, rows, :] - 7 * BLOCK
        bucket = lax.shift_right_logical(tail, 11)
        turn = -(bucket & 1) & (8 * BLOCK - 1)
        key = (bucket << 25) | ((head ^ turn) << 11) | (tail & (BLOCK - 1))
        regs.append(jnp.where(slot < live, key, DEAD))
    place = (
        [("v", k) for k in range(4)]
        + [("s", k) for k in range(3)]
        + [("v", 4)]
        + [("l", k) for k in range(7)]
    )
    regs = sort_network(regs, place, 15)
    for half in range(2):
        rows = regs[16 * half : 16 * half + 16]
        keys_ref[half] = jnp.concatenate(rows, axis=0).T
        head_row, tail_row = [], []
        least_head = least_tail = jnp.full((ROWS, LANES), 1 << 20, jnp.int32)
        most_head = most_tail = jnp.full((ROWS, LANES), -1, jnp.int32)
        for key in rows:
            used = key < DEAD
            bucket = lax.shift_right_logical(key, 25)
            head = lax.shift_right_logical(key, 18) & (LANES - 1)
            head = head ^ (-(bucket & 1) & (LANES - 1))
            least_head = jnp.minimum(least_head, jnp.where(used, head, 1 << 20))
            most_head = jnp.maximum(most_head, jnp.where(used, head, -1))
            least_tail = jnp.minimum(least_tail, jnp.where(used, bucket, 1 << 20))
            most_tail = jnp.maximum(most_tail, jnp.where(used, bucket, -1))
        for n, x in enumerate((least_head, most_head, least_tail, most_tail)):
            reduce = jnp.max if n % 2 else jnp.min
            row = 4 * half + n
            ends_ref[row : row + 1, :] = reduce(x, axis=0, keepdims=True)


def pair_sort(live, pairs):
    return pl.pallas_call(
        pair_sort_kernel,
        name="pair_sort",
        out_shape=(
            jax.ShapeDtypeStruct((2, LANES, LANES), jnp.int32),
            jax.ShapeDtypeStruct((ROWS, LANES), jnp.int32),
        ),
        in_specs=[pl.BlockSpec(memory_space=SMEM), pl.BlockSpec(memory_space=VMEM)],
        compiler_params=params(),
    )(live, pairs)


def pair_kernel(
    live_ref, ends_ref, keys_ref, own_ref, before_ref, after_ref,
    corr_ref, lower_ref, upper_ref,
    table, head_sum, tail_sum, near, far, idx, val, sems,
):
    copies = [
        pltpu.make_async_copy(before_ref, table.at[0:16], sems.at[0]),
        pltpu.make_async_copy(own_ref, table.at[16:144], sems.at[1]),
        pltpu.make_async_copy(after_ref, table.at[144:160], sems.at[2]),
    ]
    for copy in copies:
        copy.start()
    head_sum[...] = jnp.zeros_like(head_sum)
    tail_sum[...] = jnp.zeros_like(tail_sum)
    for copy in copies:
        copy.wait()
    iota16 = row_iota()
    live = live_ref[0, 0]

    def one_set(number, carry):
        half = number & 1
        first = pl.multiple_of((number >> 1) * ROWS, ROWS)
        keys = keys_ref[half, pl.ds(first, ROWS), :]
        used = keys < DEAD
        bucket = lax.shift_right_logical(keys, 25)
        odd = bucket & 1
        head = (lax.shift_right_logical(keys, 11) & (8 * BLOCK - 1)) ^ (-odd & (8 * BLOCK - 1))
        head_row = jnp.where(used, lax.shift_right_logical(head, 7), -1)
        head_low = head & (LANES - 1)
        tail_row = jnp.where(used, bucket * 16 + (lax.shift_right_logical(keys, 7) & 15), -1)
        tail_low = keys & (LANES - 1)
        idx[0] = head_row
        idx[1] = head_low
        idx[2] = tail_row
        idx[3] = tail_low
        val[0] = head_row.astype(jnp.float32)
        val[1] = head_low.astype(jnp.float32)
        val[2] = tail_row.astype(jnp.float32)
        val[3] = tail_low.astype(jnp.float32)

        head_first, tail_first = [], []
        head_span = tail_span = jnp.int32(0)
        for g in range(ROWS):
            least = ends_ref[4 * half, first + g]
            head_span = jnp.maximum(head_span, ends_ref[4 * half + 1, first + g] - least + 1)
            head_first.append(jnp.minimum(least, LANES))
            least = ends_ref[4 * half + 2, first + g]
            tail_span = jnp.maximum(tail_span, ends_ref[4 * half + 3, first + g] - least + 1)
            tail_first.append(jnp.minimum(least, 10))

        def head_trip(t, found):
            out = []
            for g in range(ROWS):
                row = jnp.broadcast_to(idx[0, g : g + 1, :], (ROWS, LANES))
                low = jnp.broadcast_to(idx[1, g : g + 1, :], (ROWS, LANES))
                base = jnp.minimum(head_first[g] + t * HEAD_STEP, LANES)
                total = found[g]
                for u in range(HEAD_STEP):
                    got = lane_gather(table[16 + base + u], low)
                    total = jnp.where(row == base + u, got, total)
                out.append(total)
            return tuple(out)

        def tail_trip(t, found):
            out = []
            for g in range(ROWS):
                row = jnp.broadcast_to(idx[2, g : g + 1, :], (ROWS, LANES))
                low = jnp.broadcast_to(idx[3, g : g + 1, :], (ROWS, LANES))
                base = jnp.minimum(tail_first[g] + t, 10) * 16
                total = found[g]
                for u in range(16):
                    got = lane_gather(table[base + u], low)
                    total = jnp.where(row == base + u, got, total)
                out.append(total)
            return tuple(out)

        blank = tuple(jnp.zeros((ROWS, LANES), jnp.float32) for _ in range(ROWS))
        got_near = lax.fori_loop(0, (head_span + HEAD_STEP - 1) // HEAD_STEP, head_trip, blank)
        got_far = lax.fori_loop(0, tail_span, tail_trip, blank)
        for g in range(ROWS):
            near[g] = got_near[g]
            far[g] = got_far[g]
        gap = jnp.zeros((ROWS, LANES), jnp.float32)
        for c in range(3):
            apart = far[:, c, :] - near[:, c, :]
            gap = gap + apart * apart
        far_radius, near_radius = far[:, 6, :], near[:, 6, :]
        far_ratio = far_radius * lax.rsqrt(gap + far_radius * far_radius)
        near_ratio = near_radius * lax.rsqrt(gap + near_radius * near_radius)
        weight_far = jnp.where(used, piep_coef * far_ratio * far_ratio * far_ratio, 0.0)
        weight_near = jnp.where(used, piep_coef * near_ratio * near_ratio * near_ratio, 0.0)
        for c in range(3):
            for n, part in enumerate(split_two(weight_far * far[:, 3 + c, :])):
                val[4 + 2 * c + n] = part
            for n, part in enumerate(split_two(weight_near * near[:, 3 + c, :])):
                val[10 + 2 * c + n] = part

        def add_heads(t, carry):
            for g in range(ROWS):
                base = jnp.minimum(head_first[g] + 16 * t, LANES)
                rel = packed_row(val.at[0], g) - base.astype(jnp.float32).astype(jnp.bfloat16)
                hot = one_hot_rows(packed_row(val.at[1], g), LANES, iota16)
                parts = [[packed_row(val.at[4 + 2 * c + n], g) for n in range(2)] for c in range(3)]
                out = lax.dot_general(
                    spread_rows(rel, parts, iota16),
                    jnp.concatenate([hot, hot], axis=1),
                    NT,
                    preferred_element_type=jnp.float32,
                )
                for c in range(3):
                    head_sum[c, pl.ds(base, 16), :] += out[16 * c : 16 * c + 16]
            return carry

        def add_tails(t, carry):
            for g in range(ROWS):
                base = jnp.minimum(tail_first[g] + t, 10) * 16
                rel = packed_row(val.at[2], g) - base.astype(jnp.float32).astype(jnp.bfloat16)
                hot = one_hot_rows(packed_row(val.at[3], g), LANES, iota16)
                parts = [[packed_row(val.at[10 + 2 * c + n], g) for n in range(2)] for c in range(3)]
                out = lax.dot_general(
                    spread_rows(rel, parts, iota16),
                    jnp.concatenate([hot, hot], axis=1),
                    NT,
                    preferred_element_type=jnp.float32,
                )
                rows = pl.ds(pl.multiple_of(base, 16), 16)
                for c in range(3):
                    tail_sum[c, rows, :] += out[16 * c : 16 * c + 16]
            return carry

        lax.fori_loop(0, (head_span + 15) // 16, add_heads, 0)
        lax.fori_loop(0, tail_span, add_tails, 0)
        return carry

    lax.fori_loop(0, 2 * ((live + 2047) // 2048), one_set, 0)
    corr_ref[...] = head_sum[:, 0:128, :] + tail_sum[:, 16:144, :]
    lower_ref[...] = tail_sum[:, 0:16, :]
    upper_ref[...] = tail_sum[:, 144:160, :]


def pair_forces(live, ends, keys, own, before, after):
    f32, i32 = jnp.float32, jnp.int32
    smem, vmem = pl.BlockSpec(memory_space=SMEM), pl.BlockSpec(memory_space=VMEM)
    hbm = pl.BlockSpec(memory_space=ANY)
    return pl.pallas_call(
        pair_kernel,
        name="pair_forces",
        out_shape=(
            jax.ShapeDtypeStruct((3, 128, LANES), f32),
            jax.ShapeDtypeStruct((3, 16, LANES), f32),
            jax.ShapeDtypeStruct((3, 16, LANES), f32),
        ),
        in_specs=[smem, smem, vmem, hbm, hbm, hbm],
        scratch_shapes=[
            VMEM((176, ROWS, LANES), f32),
            VMEM((3, 144, LANES), f32),
            VMEM((3, 176, LANES), f32),
            VMEM((ROWS, ROWS, LANES), f32),
            VMEM((ROWS, ROWS, LANES), f32),
            VMEM((4, ROWS, LANES), i32),
            VMEM((16, ROWS, LANES), f32),
            pltpu.SemaphoreType.DMA((3,)),
        ],
        compiler_params=params(),
    )(live, ends, keys, own, before, after)


def deposit_kernel(
    ends_ref, keys_ref, table_ref, corr_ref, lower_ref, upper_ref,
    out_ref, total_ref,
    cells, force, got, val,
):
    iota16 = row_iota()
    cells[...] = jnp.zeros_like(cells)
    total_ref[...] = corr_ref[...]
    total_ref[:, 0:16, :] += lower_ref[...]
    total_ref[:, 112:128, :] += upper_ref[...]

    def one_block(db, carry):
        rows = pl.ds(pl.multiple_of(db * 16, 16), 16)
        scale = (-2.0 * drag_coef) * table_ref[rows, 6, :]
        for c in range(3):
            push = scale * (table_ref[rows, 3 + c, :] + total_ref[c, rows, :])
            force[:, c, :] = push[0:8]
            force[:, 4 + c, :] = push[8:16]
        keys = keys_ref[rows, :]
        own = lax.shift_right_logical(keys, 7) & 15
        low = keys & (LANES - 1)
        tables = [force[k] for k in range(ROWS)]
        for g in range(16):
            pick = jnp.broadcast_to(own[g : g + 1, :], (ROWS, LANES))
            at = jnp.broadcast_to(low[g : g + 1, :], (ROWS, LANES))
            inner = pick & 7
            found = jnp.zeros((ROWS, LANES), jnp.float32)
            for k in range(ROWS):
                found = jnp.where(inner == k, lane_gather(tables[k], at), found)
            got[g] = jnp.where(pick >= 8, pltpu.roll(found, 4, 0), found)
        val[0] = lax.shift_right_logical(keys, 19).astype(jnp.float32)
        val[1] = (lax.shift_right_logical(keys, 11) & (2 * LANES - 1)).astype(jnp.float32)
        for c in range(3):
            for n, part in enumerate(split_two(got[:, c, :])):
                val[2 + 2 * c + n] = part
        firsts = [ends_ref[0, db * 16 + g] for g in range(16)]
        span = jnp.int32(0)
        for g in range(16):
            span = jnp.maximum(span, ends_ref[15, db * 16 + g] - firsts[g] + 1)

        def add_cells(t, carry):
            for g in range(16):
                base = jnp.minimum(firsts[g] + 16 * t, LANES)
                rel = packed_row(val.at[0], g) - base.astype(jnp.float32).astype(jnp.bfloat16)
                hot = one_hot_rows(packed_row(val.at[1], g), 2 * LANES, iota16)
                parts = [[packed_row(val.at[2 + 2 * c + n], g) for n in range(2)] for c in range(3)]
                out = lax.dot_general(
                    spread_rows(rel, parts, iota16),
                    jnp.concatenate([hot, hot], axis=1),
                    NT,
                    preferred_element_type=jnp.float32,
                )
                for c in range(3):
                    for half in range(2):
                        part = out[16 * c : 16 * c + 16, half * LANES : (half + 1) * LANES]
                        cells[2 * c + half, pl.ds(base, 16), :] += part
            return carry

        lax.fori_loop(0, (span + 15) // 16, add_cells, 0)
        return carry

    lax.fori_loop(0, 8, one_block, 0)
    for c in range(3):
        for half in range(2):
            out_ref[c, :, half * LANES : (half + 1) * LANES] = cells[2 * c + half, 0:128, :]


def deposits(ends, keys, table, corr, lower, upper):
    f32 = jnp.float32
    smem, vmem = pl.BlockSpec(memory_space=SMEM), pl.BlockSpec(memory_space=VMEM)
    return pl.pallas_call(
        deposit_kernel,
        name="deposits",
        out_shape=(
            jax.ShapeDtypeStruct((3, 128, 2 * LANES), f32),
            jax.ShapeDtypeStruct((3, 128, LANES), f32),
        ),
        in_specs=[smem, vmem, vmem, vmem, vmem, vmem],
        scratch_shapes=[
            VMEM((6, 144, LANES), f32),
            VMEM((ROWS, ROWS, LANES), f32),
            VMEM((16, ROWS, LANES), f32),
            VMEM((8, 16, LANES), f32),
        ],
        compiler_params=params(),
    )(ends, keys, table, corr, lower, upper)


def with_halo(x, sides, width, wrap):
    for axis, dim in sides:
        count, length = (lax.axis_size(axis), x.shape[dim])
        up = [(i, (i + 1) % count) for i in range(count if wrap else count - 1)]
        down = [(j, i) for i, j in up]
        last = lax.slice_in_dim(x, length - width, length, axis=dim)
        leading = lax.slice_in_dim(x, 0, width, axis=dim)
        before = lax.ppermute(last, axis, up)
        after = lax.ppermute(leading, axis, down)
        x = jnp.concatenate([before, x, after], axis=dim)
    return x


def from_behind(x, axis, by):
    count = lax.axis_size(axis)
    return lax.ppermute(x, axis, [(i, (i + by) % count) for i in range(count)])


def gauss_taps():
    offsets = jnp.arange(-2, 3).astype(jnp.float32)
    raw_taps = jnp.exp(-0.5 * offsets * offsets)
    return raw_taps / jnp.sum(raw_taps)


def taps_valid(padded, axis_number, kernel_taps):
    out_length = padded.shape[axis_number] - 4
    total = jnp.zeros(
        padded.shape[:axis_number] + (out_length,) + padded.shape[axis_number + 1 :], jnp.float32
    )
    for tap_number in range(5):
        total = total + kernel_taps[tap_number] * lax.slice_in_dim(
            padded, tap_number, tap_number + out_length, axis=axis_number
        )
    return total


def per_device(positions, velocity, diameter, cell_index, pair_list, live_pairs, gas_velocity):
    live = live_pairs.reshape(1, 1)
    table, cell_keys, cell_ends = droplet_states(
        cell_index.reshape(128, LANES),
        gas_velocity.reshape(3, 128, 2 * LANES),
        positions.reshape(3, 128, LANES),
        velocity.reshape(3, 128, LANES),
        diameter.reshape(128, LANES),
    )
    before = from_behind(table[128 - BAND_BLOCKS :], "az", 1)
    after = from_behind(table[:BAND_BLOCKS], "az", -1)
    pair_keys, pair_ends = pair_sort(live, pair_list.reshape(2, 256, LANES))
    corr, lower, upper = pair_forces(live, pair_ends, pair_keys, table, before, after)
    from_upper = from_behind(lower, "az", -1)
    from_lower = from_behind(upper, "az", 1)
    deposit, correction = deposits(cell_ends, cell_keys, table, corr, from_lower, from_upper)
    deposit = deposit.reshape(gas_velocity.shape)
    kernel_taps = gauss_taps()
    padded = with_halo(deposit, (("ax", 1), ("rad", 2)), 2, False)
    padded = with_halo(padded, (("az", 3),), 2, True)
    smoothed = taps_valid(padded, 1, kernel_taps)
    smoothed = taps_valid(smoothed, 2, kernel_taps)
    smoothed = taps_valid(smoothed, 3, kernel_taps)
    return (correction.reshape(positions.shape), smoothed)


def solution(mesh):
    return jax.shard_map(
        per_device,
        mesh=mesh,
        in_specs=(
            P(None, "ax", "rad", "az"),
            P(None, "ax", "rad", "az"),
            P("ax", "rad", "az"),
            P("ax", "rad", "az"),
            P(None, "ax", "rad", "az"),
            P("ax", "rad", "az"),
            P(None, "ax", "rad", "az"),
        ),
        out_specs=(P(None, "ax", "rad", "az"), P(None, "ax", "rad", "az")),
        check_vma=False,
    )
```

time: 1250 us -> 177 us (0.14)
  the two profiles are of different devices: /device:TPU:40 before, /device:TPU:48 now
where the time goes in v1:
time: 177 us
  Pallas kernels  64.5 us (36%)
  waiting for transfers between devices  50.9 us (29%)
  starting transfers between devices  40.9 us (23%)
  other arithmetic  13.5 us (8%)
  local copies, waits for them, and re-layouts  5.4 us (3%)
    pallas_call x1, Pallas kernels, pair_forces(): pl.pallas_call(pair_kernel, name='pair_forces', out_shape=(jax.ShapeDtype...  34 us
    ppermute x3, waiting for transfers between devices, with_halo(): after = lax.ppermute(leading, axis, down)  27.3 us
    ppermute x3, waiting for transfers between devices, with_halo(): before = lax.ppermute(last, axis, up)  18.7 us
    ppermute x4, starting transfers between devices, from_behind(): return lax.ppermute(x, axis, [(i, (i + by) % count) for i in range(count)])  16.5 us
    pallas_call x1, Pallas kernels, droplet_states(): pl.pallas_call(droplet_kernel, name='droplet_states', out_shape=(jax.Shap...  16.4 us
    ppermute x3, starting transfers between devices, with_halo(): after = lax.ppermute(leading, axis, down)  14.4 us
    add x3, other arithmetic, taps_valid(): total + kernel_taps[tap_number] * lax.slice_in_dim(padded, tap_number, ta...  11.2 us
    pallas_call x1, Pallas kernels, deposits(): pl.pallas_call(deposit_kernel, name='deposits', out_shape=(jax.ShapeDtype...  10.5 us
  transfers between devices with their start and end apart: 10, of which 6 were waited for; matrix products, arithmetic and copies ran while one was open for 1% of the time, Pallas kernels for 2%

profile of v1, /device:TPU:48, one launch (start us, length us, event | category | flops | bytes accessed | tf_op | source)
XLA Modules:
  0.0 176.6 jit_solution(11684724370527468160)
XLA Ops:
  0.6 1.0 copy-done
  1.6 0.9 copy-done.2
  2.6 0.9 copy-done.3
  3.5 0.8 copy-done.4
  4.3 0.8 copy-done.5
  5.2 16.4 %droplet_states.1 = (f32[128,8,128]{2,1,0:T(8,128)S(1)}, s32[128,128]{1,0:T(8,128)S(1)}, s32[16,128]{1,0:T(8,128)S(1)}) custom-call(s32[128,128]{1,0:T(8,128)S(1)} %bitcast.24, f32[3,128,256]{2,1,0:T(8,128)S(1)} %bitcast.20, f32[3,128,128]{2,1,0:T(8,128)S(1)} %bitcast.22, f32[3,128,128]{2,1,0:T(8,128)S(1)} %bitcast.23, f32[128,128]{1,0:T(8,128)S(1)} %bitcast.25), custom_call_target="tpu_custom_call" | custom-call | tf_op jit(solution)/shard_map/droplet_states/pallas_call | solution.py:217
  21.6 6.6 %collective-permute-start = (f32[16,8,128]{2,1,0:T(8,128)S(1)}, f32[16,8,128]{2,1,0:T(8,128)S(1)}, u32[]{:S(2)}, u32[]{:S(2)}) collective-permute-start(f32[16,8,128]{2,1,0:T(8,128)S(1)} %get-tuple-element.31), channel_id=1, source_target_pairs={{0,1},{1,2},{2,3},{3,4},{4,5},{5,6},{6,7},{7,0},{8,9},{9,10},{10,1... | collective-permute-start | bytes 196616 | tf_op jit(solution)/shard_map/ppermute | solution.py:563
  28.1 1.8 %collective-permute-start.1 = (f32[16,8,128]{2,1,0:T(8,128)S(1)}, f32[16,8,128]{2,1,0:T(8,128)S(1)}, u32[]{:S(2)}, u32[]{:S(2)}) collective-permute-start(f32[16,8,128]{2,1,0:T(8,128)S(1)} %get-tuple-element.30), channel_id=1, source_target_pairs={{0,7},{1,0},{2,1},{3,2},{4,3},{5,4},{6,5},{7,6},{8,15},{9,8},{10,9... | collective-permute-start | bytes 196616 | tf_op jit(solution)/shard_map/ppermute | solution.py:563
  30.7 3.7 %pair_sort.1 = (s32[2,128,128]{2,1,0:T(8,128)S(1)}, s32[8,128]{1,0:T(8,128)S(1)}) custom-call(s32[1,1]{1,0:T(1,128)} %bitcast.14.live_ref, s32[2,256,128]{2,1,0:T(8,128)S(1)} %bitcast.21), custom_call_target="tpu_custom_call" | custom-call | tf_op jit(solution)/shard_map/pair_sort/pallas_call | solution.py:281
  34.4 3.1 %collective-permute-done.1.after_ref = f32[16,8,128]{2,1,0:T(8,128)S(1)} collective-permute-done((f32[16,8,128]{2,1,0:T(8,128)S(1)}, f32[16,8,128]{2,1,0:T(8,128)S(1)}, u32[]{:S(2)}, u32[]{:S(2)}) %collective-permute-start.1) | collective-permute-done | bytes 65568 | tf_op jit(solution)/shard_map/ppermute | solution.py:563
  37.5 34.0 %pair_forces.1 = (f32[3,128,128]{2,1,0:T(8,128)S(1)}, f32[3,16,128]{2,1,0:T(8,128)S(1)}, f32[3,16,128]{2,1,0:T(8,128)S(1)}) custom-call(s32[1,1]{1,0:T(1,128)} %bitcast.15.live_ref, s32[8,128]{1,0:T(8,128)S(1)} %get-tuple-element.15.ends_ref, s32[2,128,128]{2,1,0:T(8,128)S(1)} %get-tuple-element.16.keys_ref, ...), custom_call_target="tpu_custom_call" | custom-call | tf_op jit(solution)/shard_map/pair_forces/pallas_call | solution.py:437
  71.6 8.0 %collective-permute-start.3 = (f32[3,16,128]{2,1,0:T(8,128)S(1)}, f32[3,16,128]{2,1,0:T(8,128)S(1)}, u32[]{:S(2)}, u32[]{:S(2)}) collective-permute-start(f32[3,16,128]{2,1,0:T(8,128)S(1)} %get-tuple-element.19), channel_id=1, source_target_pairs={{0,7},{1,0},{2,1},{3,2},{4,3},{5,4},{6,5},{7,6},{8,15},{9,8},{10,9... | collective-permute-start | bytes 73736 | tf_op jit(solution)/shard_map/ppermute | solution.py:563
  79.6 1.8 %collective-permute-done.2.lower_ref = f32[3,16,128]{2,1,0:T(8,128)S(1)} collective-permute-done((f32[3,16,128]{2,1,0:T(8,128)S(1)}, f32[3,16,128]{2,1,0:T(8,128)S(1)}, u32[]{:S(2)}, u32[]{:S(2)}) %collective-permute-start.2) | collective-permute-done | bytes 24608 | tf_op jit(solution)/shard_map/ppermute | solution.py:563
  81.4 10.5 %deposits.1 = (f32[3,128,256]{2,1,0:T(8,128)S(1)}, f32[3,128,128]{2,1,0:T(8,128)}) custom-call(s32[16,128]{1,0:T(8,128)S(1)} %get-tuple-element.12.ends_ref, s32[128,128]{1,0:T(8,128)S(1)} %get-tuple-element.13.keys_ref, f32[128,8,128]{2,1,0:T(8,128)S(1)} %get-tuple-element.14.own_ref.table_ref, f32[3,128,128]{2,1,0:T(8,128)S(1)} %get-tuple-element.17.corr_ref, ...), custom_call_target="tpu_custom_call" | custom-call | tf_op jit(solution)/shard_map/deposits/pallas_call | solution.py:530
  91.9 5.2 %collective-permute-start.5 = (f32[3,2,16,256]{3,2,1,0:T(8,128)S(1)}, f32[3,2,16,256]{3,2,1,0:T(8,128)S(1)}, u32[]{:S(2)}, u32[]{:S(2)}) collective-permute-start(f32[3,2,16,256]{3,2,1,0:T(8,128)S(1)} %get-tuple-element.33), channel_id=1, source_target_pairs={{64,0},{128,64},{192,128},{65,1},{129,65},{193,129},{66,2},{130,66... | collective-permute-start | bytes 294920 | tf_op jit(solution)/shard_map/ppermute | solution.py:556
  97.1 4.5 %collective-permute-start.4 = (f32[3,2,16,256]{3,2,1,0:T(8,128)S(1)}, f32[3,2,16,256]{3,2,1,0:T(8,128)S(1)}, u32[]{:S(2)}, u32[]{:S(2)}) collective-permute-start(f32[3,2,16,256]{3,2,1,0:T(8,128)S(1)} %get-tuple-element.32), channel_id=1, source_target_pairs={{0,64},{64,128},{128,192},{1,65},{65,129},{129,193},{2,66},{66,130... | collective-permute-start | bytes 294920 | tf_op jit(solution)/shard_map/ppermute | solution.py:555
  101.5 0.6 fusion.13
  102.2 1.4 collective-permute-done.4
  103.6 6.7 %collective-permute-start.7 = (f32[3,12,2,256]{3,2,1,0:T(2,128)S(1)}, f32[3,12,2,256]{3,2,1,0:T(2,128)S(1)}, u32[]{:S(2)}, u32[]{:S(2)}) collective-permute-start(f32[3,12,2,256]{3,2,1,0:T(2,128)S(1)} %get-tuple-element.29), channel_id=1, source_target_pairs={{8,0},{16,8},{24,16},{32,24},{40,32},{48,40},{56,48},{9,1},{17,9},... | collective-permute-start | bytes 221192 | tf_op jit(solution)/shard_map/ppermute | solution.py:556
  110.4 1.9 %collective-permute-start.6 = (f32[3,12,2,256]{3,2,1,0:T(2,128)S(1)}, f32[3,12,2,256]{3,2,1,0:T(2,128)S(1)}, u32[]{:S(2)}, u32[]{:S(2)}) collective-permute-start(f32[3,12,2,256]{3,2,1,0:T(2,128)S(1)} %get-tuple-element.28), channel_id=1, source_target_pairs={{0,8},{8,16},{16,24},{24,32},{32,40},{40,48},{48,56},{1,9},{9,17},... | collective-permute-start | bytes 221192 | tf_op jit(solution)/shard_map/ppermute | solution.py:555
  112.3 0.7 broadcast_divide_fusion
  113.0 6.2 %collective-permute-done.6 = f32[3,12,2,256]{3,2,1,0:T(2,128)S(1)} collective-permute-done((f32[3,12,2,256]{3,2,1,0:T(2,128)S(1)}, f32[3,12,2,256]{3,2,1,0:T(2,128)S(1)}, u32[]{:S(2)}, u32[]{:S(2)}) %collective-permute-start.6) | collective-permute-done | bytes 73760 | tf_op jit(solution)/shard_map/ppermute | solution.py:555
  119.3 0.2 fusion.14
  119.5 2.4 %collective-permute-start.9 = (f32[3,12,20,2]{3,2,1,0:T(8,128)S(1)}, f32[3,12,20,2]{3,2,1,0:T(8,128)S(1)}, u32[]{:S(2)}, u32[]{:S(2)}) collective-permute-start(f32[3,12,20,2]{3,2,1,0:T(8,128)S(1)} %get-tuple-element.27), channel_id=1, source_target_pairs={{1,0},{2,1},{3,2},{4,3},{5,4},{6,5},{7,6},{0,7},{9,8},{10,9},{11,1... | collective-permute-start | bytes 17288 | tf_op jit(solution)/shard_map/ppermute | solution.py:556
  121.9 3.6 %collective-permute-start.8 = (f32[3,12,20,2]{3,2,1,0:T(8,128)S(1)}, f32[3,12,20,2]{3,2,1,0:T(8,128)S(1)}, u32[]{:S(2)}, u32[]{:S(2)}) collective-permute-start(f32[3,12,20,2]{3,2,1,0:T(8,128)S(1)} %get-tuple-element.26), channel_id=1, source_target_pairs={{0,1},{1,2},{2,3},{3,4},{4,5},{5,6},{6,7},{7,0},{8,9},{9,10},{10,1... | collective-permute-start | bytes 17288 | tf_op jit(solution)/shard_map/ppermute | solution.py:555
  125.5 0.7 fusion.17
  126.2 27.3 %collective-permute-done.9 = f32[3,12,20,2]{3,2,1,0:T(8,128)S(1)} collective-permute-done((f32[3,12,20,2]{3,2,1,0:T(8,128)S(1)}, f32[3,12,20,2]{3,2,1,0:T(8,128)S(1)}, u32[]{:S(2)}, u32[]{:S(2)}) %collective-permute-start.9) | collective-permute-done | bytes 5792 | tf_op jit(solution)/shard_map/ppermute | solution.py:556
  153.4 11.1 %collective-permute-done.8 = f32[3,12,20,2]{3,2,1,0:T(8,128)S(1)} collective-permute-done((f32[3,12,20,2]{3,2,1,0:T(8,128)S(1)}, f32[3,12,20,2]{3,2,1,0:T(8,128)S(1)}, u32[]{:S(2)}, u32[]{:S(2)}) %collective-permute-start.8) | collective-permute-done | bytes 5792 | tf_op jit(solution)/shard_map/ppermute | solution.py:555
  164.6 0.8 pad_maximum_fusion
  165.4 3.4 %fusion = f32[3,8,20,260]{3,2,1,0:T(8,128)S(1)} fusion(f32[3,12,20,260]{3,2,1,0:T(8,128)S(1)} %pad_maximum_fusion, f32[]{:T(128)} %bitcast.13, f32[]{:T(128)} %bitcast.12, f32[]{:T(128)} %bitcast.11, f32[]{:T(128)} %bitcast.10, f32[]{:T(128)} %bitcast.8), kind=kLoop, calls=%fused_computation.2 | loop fusion | flops 1123200 | bytes 2995220 | tf_op jit(solution)/shard_map/add | solution.py:578
  168.8 3.5 %fusion.4 = f32[3,8,16,260]{3,2,1,0:T(8,128)S(1)} fusion(f32[3,8,20,260]{3,2,1,0:T(8,128)S(1)} %fusion, f32[]{:T(128)} %bitcast.13, f32[]{:T(128)} %bitcast.12, f32[]{:T(128)} %bitcast.11, f32[]{:T(128)} %bitcast.10, f32[]{:T(128)} %bitcast.8), kind=kLoop, calls=%fused_computation.12 | loop fusion | flops 898560 | bytes 2396180 | tf_op jit(solution)/shard_map/add | solution.py:578
  172.2 4.4 %fusion.8 = f32[3,8,16,256]{3,2,1,0:T(8,128)} fusion(f32[3,8,16,260]{3,2,1,0:T(8,128)S(1)} %fusion.4, f32[]{:T(128)} %bitcast.13, f32[]{:T(128)} %bitcast.12, f32[]{:T(128)} %bitcast.11, f32[]{:T(128)} %bitcast.10, f32[]{:T(128)} %bitcast.8), kind=kLoop, calls=%fused_computation.21 | loop fusion | flops 884736 | bytes 2359316 | tf_op jit(solution)/shard_map/add | solution.py:578
  (16 shorter events, 0.3 us)
Async XLA Ops:
  0.6 1.0 copy-start
  1.6 0.9 copy-start.2
  2.6 0.9 copy-start.3
  3.5 0.8 copy-start.4
  4.3 0.8 copy-start.5
  5.2 25.5 %copy-start.1 = (s32[2,1,1,32768]{3,2,1,0:T(1,128)S(1)}, s32[2,1,1,32768]{3,2,1,0:T(1,128)}, u32[]{:S(2)}) copy-start(s32[2,1,1,32768]{3,2,1,0:T(1,128)} %param.11) | copy-start | bytes 786436
  21.6 12.8 %collective-permute-start = (f32[16,8,128]{2,1,0:T(8,128)S(1)}, f32[16,8,128]{2,1,0:T(8,128)S(1)}, u32[]{:S(2)}, u32[]{:S(2)}) collective-permute-start(f32[16,8,128]{2,1,0:T(8,128)S(1)} %get-tuple-element.31), channel_id=1, source_target_pairs={{0,1},{1,2},{2,3},{3,4},{4,5},{5,6},{6,7},{7,0},{8,9},{9,10},{10,1... | collective-permute-start | bytes 196616 | tf_op jit(solution)/shard_map/ppermute | solution.py:563
  28.1 9.3 %collective-permute-start.1 = (f32[16,8,128]{2,1,0:T(8,128)S(1)}, f32[16,8,128]{2,1,0:T(8,128)S(1)}, u32[]{:S(2)}, u32[]{:S(2)}) collective-permute-start(f32[16,8,128]{2,1,0:T(8,128)S(1)} %get-tuple-element.30), channel_id=1, source_target_pairs={{0,7},{1,0},{2,1},{3,2},{4,3},{5,4},{6,5},{7,6},{8,15},{9,8},{10,9... | collective-permute-start | bytes 196616 | tf_op jit(solution)/shard_map/ppermute | solution.py:563
  71.5 9.9 %collective-permute-start.2 = (f32[3,16,128]{2,1,0:T(8,128)S(1)}, f32[3,16,128]{2,1,0:T(8,128)S(1)}, u32[]{:S(2)}, u32[]{:S(2)}) collective-permute-start(f32[3,16,128]{2,1,0:T(8,128)S(1)} %get-tuple-element.18), channel_id=1, source_target_pairs={{0,1},{1,2},{2,3},{3,4},{4,5},{5,6},{6,7},{7,0},{8,9},{9,10},{10,1... | collective-permute-start | bytes 73736 | tf_op jit(solution)/shard_map/ppermute | solution.py:563
  71.6 9.8 %collective-permute-start.3 = (f32[3,16,128]{2,1,0:T(8,128)S(1)}, f32[3,16,128]{2,1,0:T(8,128)S(1)}, u32[]{:S(2)}, u32[]{:S(2)}) collective-permute-start(f32[3,16,128]{2,1,0:T(8,128)S(1)} %get-tuple-element.19), channel_id=1, source_target_pairs={{0,7},{1,0},{2,1},{3,2},{4,3},{5,4},{6,5},{7,6},{8,15},{9,8},{10,9... | collective-permute-start | bytes 73736 | tf_op jit(solution)/shard_map/ppermute | solution.py:563
  91.9 10.3 %collective-permute-start.5 = (f32[3,2,16,256]{3,2,1,0:T(8,128)S(1)}, f32[3,2,16,256]{3,2,1,0:T(8,128)S(1)}, u32[]{:S(2)}, u32[]{:S(2)}) collective-permute-start(f32[3,2,16,256]{3,2,1,0:T(8,128)S(1)} %get-tuple-element.33), channel_id=1, source_target_pairs={{64,0},{128,64},{192,128},{65,1},{129,65},{193,129},{66,2},{130,66... | collective-permute-start | bytes 294920 | tf_op jit(solution)/shard_map/ppermute | solution.py:556
  97.1 6.5 %collective-permute-start.4 = (f32[3,2,16,256]{3,2,1,0:T(8,128)S(1)}, f32[3,2,16,256]{3,2,1,0:T(8,128)S(1)}, u32[]{:S(2)}, u32[]{:S(2)}) collective-permute-start(f32[3,2,16,256]{3,2,1,0:T(8,128)S(1)} %get-tuple-element.32), channel_id=1, source_target_pairs={{0,64},{64,128},{128,192},{1,65},{65,129},{129,193},{2,66},{66,130... | collective-permute-start | bytes 294920 | tf_op jit(solution)/shard_map/ppermute | solution.py:555
  103.6 9.3 %collective-permute-start.7 = (f32[3,12,2,256]{3,2,1,0:T(2,128)S(1)}, f32[3,12,2,256]{3,2,1,0:T(2,128)S(1)}, u32[]{:S(2)}, u32[]{:S(2)}) collective-permute-start(f32[3,12,2,256]{3,2,1,0:T(2,128)S(1)} %get-tuple-element.29), channel_id=1, source_target_pairs={{8,0},{16,8},{24,16},{32,24},{40,32},{48,40},{56,48},{9,1},{17,9},... | collective-permute-start | bytes 221192 | tf_op jit(solution)/shard_map/ppermute | solution.py:556
  110.4 8.8 %collective-permute-start.6 = (f32[3,12,2,256]{3,2,1,0:T(2,128)S(1)}, f32[3,12,2,256]{3,2,1,0:T(2,128)S(1)}, u32[]{:S(2)}, u32[]{:S(2)}) collective-permute-start(f32[3,12,2,256]{3,2,1,0:T(2,128)S(1)} %get-tuple-element.28), channel_id=1, source_target_pairs={{0,8},{8,16},{16,24},{24,32},{32,40},{40,48},{48,56},{1,9},{9,17},... | collective-permute-start | bytes 221192 | tf_op jit(solution)/shard_map/ppermute | solution.py:555
  119.5 33.9 %collective-permute-start.9 = (f32[3,12,20,2]{3,2,1,0:T(8,128)S(1)}, f32[3,12,20,2]{3,2,1,0:T(8,128)S(1)}, u32[]{:S(2)}, u32[]{:S(2)}) collective-permute-start(f32[3,12,20,2]{3,2,1,0:T(8,128)S(1)} %get-tuple-element.27), channel_id=1, source_target_pairs={{1,0},{2,1},{3,2},{4,3},{5,4},{6,5},{7,6},{0,7},{9,8},{10,9},{11,1... | collective-permute-start | bytes 17288 | tf_op jit(solution)/shard_map/ppermute | solution.py:556
  121.9 42.6 %collective-permute-start.8 = (f32[3,12,20,2]{3,2,1,0:T(8,128)S(1)}, f32[3,12,20,2]{3,2,1,0:T(8,128)S(1)}, u32[]{:S(2)}, u32[]{:S(2)}) collective-permute-start(f32[3,12,20,2]{3,2,1,0:T(8,128)S(1)} %get-tuple-element.26), channel_id=1, source_target_pairs={{0,1},{1,2},{2,3},{3,4},{4,5},{5,6},{6,7},{7,0},{8,9},{9,10},{10,1... | collective-permute-start | bytes 17288 | tf_op jit(solution)/shard_map/ppermute | solution.py:555
